TPU v7x, 32 devices: a whole 2x2x4 slice. The times are simulated.
32 devices in a mesh: inst: 8 (over y, x, core), mesh: 4 (over z).
Axes of the slice: x: 2, y: 2, z: 4, core: 2. Of those that a mesh axis runs over, the one named last changes fastest.
Arguments:
- state: float32 [16, 128, 5, 128], P('inst', 'mesh'), may hold values from -6 to 6
- cell_block: float32 [16, 128, 5, 5, 128], P('inst', 'mesh'), may hold values from -3 to 3
- face_block: float32 [16, 128, 6, 5, 5, 128], P('inst', 'mesh'), may hold values from -1.8 to 1.8
- neighbor: int32 [128, 6], P('mesh'), may hold values from 0 to 47
- face_cell: int32 [128, 6, 128], P('mesh'), may hold values from 0 to 127
- send_list: int32 [4, 2, 8], P('mesh'), may hold values from 0 to 31
- send_count: int32 [4, 2], P('mesh'), may hold values from 1 to 8, as said below
Outputs:
- product: float32 [16, 128, 5, 128], P('inst', 'mesh')
Inputs may be any that keep to these rules, and one draw needn't show every extreme that they name: `send_count`: the first partition always sends 8 tiles to its lower neighbour.
All inputs are finite; a program needn't handle non-finite values.
Results may differ from a plain program's by a relative error of at most 0.0003.
Values sent between devices are 32-bit elements; how exact they have to be, the bound alone decides.
A program may use at most 128 MiB of HBM per device.

v0:
```python
import math

import jax
import jax.numpy as jnp
from jax import lax
from jax.sharding import PartitionSpec as P

INST = 16
NVAR = 5
TILE = 128


DISSIPATION = 0.05


def from_behind(value, axis, steps):
    count = lax.axis_size(axis)
    pairs = [(source, (source + steps) % count) for source in range(count)]
    return lax.ppermute(value, axis, pairs)


def spectral_matrix(count):
    row_index = jnp.arange(count, dtype=jnp.int32)[:, None]
    col_index = jnp.arange(count, dtype=jnp.int32)[None, :]
    offset = row_index - col_index
    angle = math.pi / count * offset.astype(jnp.float32)
    parity = (1 - 2 * (offset % 2)).astype(jnp.float32)
    sine_safe = jnp.where(offset == 0, jnp.float32(1.0), jnp.sin(angle))
    first_order = 0.5 * parity * jnp.cos(angle) / sine_safe
    second_order = -0.5 * parity / (sine_safe * sine_safe)
    values = first_order + DISSIPATION * second_order
    diagonal_value = jnp.float32(-DISSIPATION * (count * count + 2) / 12.0)
    return jnp.where(offset == 0, diagonal_value, values)


def fetch(buffer, slots, cells):
    inst_rows = buffer.shape[0]
    total_tiles = buffer.shape[1]
    flattened = jnp.transpose(buffer, (0, 2, 1, 3)).reshape(inst_rows, NVAR, total_tiles * TILE)
    indices = (slots[:, :, None] * TILE + cells).reshape(-1)
    facing = jnp.take(flattened, indices, axis=2)
    facing = facing.reshape(inst_rows, NVAR, slots.shape[0], slots.shape[1], TILE)
    return jnp.transpose(facing, (0, 2, 3, 1, 4))


def couple(blocks, facing):
    return jnp.sum(blocks * facing[:, :, :, None], axis=(2, 4))


def packet(state, listed, count_now):
    picked = jnp.take(state, listed, axis=1)
    active = jnp.arange(listed.shape[0], dtype=jnp.int32) < count_now
    return jnp.where(active[None, :, None, None], picked, 0.0)


def shards(state, cell_block, face_block, neighbor, face_cell, send_list, send_count):
    inst_rows = state.shape[0]
    dmatrix = spectral_matrix(INST)
    first_own = lax.axis_index("inst") * inst_rows
    upward = packet(state, send_list[0, 1], send_count[0, 1])
    downward = packet(state, send_list[0, 0], send_count[0, 0])
    from_lower = from_behind(upward, "mesh", 1)
    from_upper = from_behind(downward, "mesh", -1)
    piece = lax.all_gather(state, "inst", axis=0, tiled=True)
    columns = lax.dynamic_slice(dmatrix, (first_own, 0), (inst_rows, piece.shape[0]))
    spectral = jnp.einsum("nm,mtac->ntac", columns, piece, precision=lax.Precision.HIGHEST)
    cell_term = jnp.sum(cell_block * state[:, :, None], axis=3)
    buffer = jnp.concatenate([state, from_lower, from_upper], axis=1)
    face_term = couple(face_block, fetch(buffer, neighbor, face_cell))
    return spectral + cell_term + face_term


def solution(mesh):
    placed = (
        P("inst", "mesh", None, None),
        P("inst", "mesh", None, None, None),
        P("inst", "mesh", None, None, None, None),
        P("mesh", None),
        P("mesh", None, None),
        P("mesh", None, None),
        P("mesh", None),
    )
    return jax.shard_map(
        shards, mesh=mesh, in_specs=placed, out_specs=P("inst", "mesh", None, None), check_vma=False
    )
```

profile of v0, /device:TPU:0, one launch (start us, length us, event | category | flops | bytes accessed | tf_op | source)
XLA Modules:
  0.0 239.1 jit_solution(8165604803707141801)
XLA Ops:
  6.5 0.0 copy-start
  6.5 0.0 copy-start.2
  6.5 0.0 copy-start.1
  6.5 0.0 all-gather.2.cloned.1.call-start
  6.5 0.7 all-gather.2.cloned.1.call-update
  7.3 1.3 fusion.31
  8.6 1.5 compare_and_fusion.2
  10.0 1.5 gather_fusion.2
  11.6 0.1 bitcast_select_fusion
  11.7 5.0 %collective-permute-start.1 = (f32[2,8,5,128]{3,1,2,0:T(8,128)S(1)}, f32[2,8,5,128]{3,1,2,0:T(8,128)S(1)}, u32[]{:S(2)}, u32[]{:S(2)}) collective-permute-start(f32[2,8,5,128]{3,1,2,0:T(8,128)S(1)} %bitcast_select_fusion), channel_id=1, source_target_pairs={{0,3},{1,0},{2,1},{3,2},{4,7},{5,4},{6,5},{7,6},{8,11},{9,8},{10,9... | collective-permute-start | bytes 122888 | tf_op jit(solution)/shard_map/ppermute | solution.py:19
  16.7 1.5 gather_fusion.1
  18.2 0.7 iota_compare_fusion.1
  18.9 0.1 bitcast_select_fusion.1
  19.0 0.0 collective-permute-start
  19.0 0.7 broadcast_multiply_fusion
  19.7 0.0 copy-done.2
  19.7 0.1 compare_and_fusion
  19.8 0.1 copy.32
  19.9 0.1 reshape.61
  20.0 0.1 compare_select_fusion
  20.1 0.1 convert_multiply_fusion
  20.2 0.0 copy-done
  20.2 0.0 copy-done.1
  20.2 0.1 multiply_reduce_fusion.1
  20.4 0.0 collective-permute-done.1
  20.4 4.4 %collective-permute-done = f32[2,8,5,128]{3,1,2,0:T(8,128)S(1)} collective-permute-done((f32[2,8,5,128]{3,1,2,0:T(8,128)S(1)}, f32[2,8,5,128]{3,1,2,0:T(8,128)S(1)}, u32[]{:S(2)}, u32[]{:S(2)}) %collective-permute-start) | collective-permute-done | bytes 40992 | tf_op jit(solution)/shard_map/ppermute | solution.py:19
  24.8 4.5 %copy.40 = f32[2,5,48,128]{1,0,3,2:T(2,128)} copy(f32[2,5,48,128]{3,2,1,0:T(8,128)S(1)} %maximum_bitcast_fusion) | data formatting | bytes 491520 | tf_op jit(solution)/shard_map/reshape | solution.py:39
  29.3 171.0 %gather_fusion = f32[24576,2,5]{2,1,0:T(2,128)} fusion(f32[2,5,6144]{1,0,2:T(2,128)} %bitcast.27, s32[24576]{0:T(1024)S(1)} %broadcast_clamp_fusion), kind=kCustom, calls=%fused_computation.2 | custom fusion | bytes 2064384 | tf_op jit(solution)/shard_map/jit(_take)/gather | solution.py:41
  200.3 24.8 %copy.39 = f32[2,5,32,6,128]{4,3,2,0,1:T(8,128)S(1)} copy(f32[2,5,32,6,128]{1,0,4,3,2:T(2,128)} %bitcast.26) | data formatting | bytes 1966080 | tf_op jit(solution)/shard_map/jit(_take)/gather | solution.py:41
  225.1 0.1 select_bitcast_fusion
  225.3 0.2 copy.35
  225.5 3.1 %multiply_reduce_fusion = f32[2,32,5,128]{3,1,2,0:T(8,128)S(1)} fusion(f32[2,32,6,5,5,128]{5,1,4,3,2,0:T(8,128)} %param.11, f32[2,32,6,5,128]{4,1,3,2,0:T(8,128)S(1)} %copy.35), kind=kLoop, calls=%fused_computation.3 | loop fusion | flops 2416640 | bytes 6062080 | tf_op jit(solution)/shard_map/reduce_sum | solution.py:47
  228.6 0.0 all-gather.2.cloned.1.call-done
  228.6 2.9 %fusion = f32[2,32,5,128]{3,0,2,1:T(2,128)S(1)} fusion(f32[16,32,5,128]{3,1,2,0:T(8,128)} %all-gather.2.cloned.1.call-done, f32[16,16]{1,0:T(8,128)S(1)} %get-tuple-element.17, s32[]{:T(128)S(6)} %select_n.56, f32[16,16]{1,0:T(8,128)S(1)} %get-tuple-element.18, pred[16,16]{1,0:T(8,128)(4,1)S(1)} %fusion.6, s32[16,16]{1,0:T(8,128)S(1)} %fusion.5), kind=kOutput, calls=%fused_computation.4 | convolution fusion | flops 7864672 | bytes 1478148 | tf_op jit(solution)/shard_map/nm,mtac->ntac/dot_general | solution.py:66
  231.6 0.7 fusion.2
  (7 shorter events, 0.1 us)
Async XLA Ops:
  6.5 13.6 %copy-start = (f32[2,32,5,128]{3,1,2,0:T(8,128)S(1)}, f32[2,32,5,128]{3,1,2,0:T(8,128)}, u32[]{:S(2)}) copy-start(f32[2,32,5,128]{3,1,2,0:T(8,128)} %param.9) | copy-start | bytes 491524
  6.5 13.1 %copy-start.2 = (s32[32,6,128]{2,0,1:T(8,128)S(1)}, s32[32,6,128]{2,0,1:T(8,128)}, u32[]{:S(2)}) copy-start(s32[32,6,128]{2,0,1:T(8,128)} %param.13) | copy-start | bytes 294916
  6.5 13.6 %copy-start.1 = (f32[2,32,5,5,128]{4,1,3,2,0:T(8,128)S(1)}, f32[2,32,5,5,128]{4,1,3,2,0:T(8,128)}, u32[]{:S(2)}) copy-start(f32[2,32,5,5,128]{4,1,3,2,0:T(8,128)} %param.10) | copy-start | bytes 2457604
  6.5 222.1 %all-gather.2.cloned.1.call-start = ((), (), s32[]{:S(2)}) async-start(), calls=%async_computation | async-start | bytes 1474560 | tf_op jit(solution)/shard_map/all_gather | solution.py:64
  11.7 8.7 %collective-permute-start.1 = (f32[2,8,5,128]{3,1,2,0:T(8,128)S(1)}, f32[2,8,5,128]{3,1,2,0:T(8,128)S(1)}, u32[]{:S(2)}, u32[]{:S(2)}) collective-permute-start(f32[2,8,5,128]{3,1,2,0:T(8,128)S(1)} %bitcast_select_fusion), channel_id=1, source_target_pairs={{0,3},{1,0},{2,1},{3,2},{4,7},{5,4},{6,5},{7,6},{8,11},{9,8},{10,9... | collective-permute-start | bytes 122888 | tf_op jit(solution)/shard_map/ppermute | solution.py:19
  19.0 5.8 %collective-permute-start = (f32[2,8,5,128]{3,1,2,0:T(8,128)S(1)}, f32[2,8,5,128]{3,1,2,0:T(8,128)S(1)}, u32[]{:S(2)}, u32[]{:S(2)}) collective-permute-start(f32[2,8,5,128]{3,1,2,0:T(8,128)S(1)} %bitcast_select_fusion.1), channel_id=1, source_target_pairs={{0,1},{1,2},{2,3},{3,0},{4,5},{5,6},{6,7},{7,4},{8,9},{9,10},{10,1... | collective-permute-start | bytes 122888 | tf_op jit(solution)/shard_map/ppermute | solution.py:19
Sparse Core Ops, SparseCore 0:
  9.2 27.2 all-gather.1
where the time goes:
time: 240 us; the launch traced here: 239 us
  local copies, waits for them, and re-layouts  205 us (85%)
  between operations  13.6 us (6%)
  other arithmetic  7.34 us (3%)
  waiting for transfers between devices  5.15 us (2%)
  starting transfers between devices  5.05 us (2%)
  matrix products  2.93 us (1%)
    gather x2, local copies, waits for them, and re-layouts, fetch(): facing = jnp.take(flattened, indices, axis=2)  196 us
    ppermute x2, starting transfers between devices, from_behind(): return lax.ppermute(value, axis, pairs)  5.05 us
  transfers between devices with their start and end apart: 3, of which 1 were waited for; matrix products, arithmetic and copies ran while one was open for 89% of the time, Pallas kernels for 0%

commit v1 on v0

v1 whole, which is shorter than its diff:
```python
import functools
import math

import jax
import jax.numpy as jnp
from jax import lax
from jax.experimental import pallas as pl
from jax.experimental.pallas import tpu as pltpu
from jax.sharding import PartitionSpec as P

DISSIPATION = 0.05
LANES = 128
ROWS = 8
MESH = pl.DeviceIdType.MESH


def spectral_coefficient(offset, count):
    offset = offset % count
    if offset == 0:
        return -DISSIPATION * (count * count + 2) / 12.0
    angle = math.pi * offset / count
    parity = 1 - 2 * (offset % 2)
    sine = math.sin(angle)
    return 0.5 * parity * math.cos(angle) / sine - DISSIPATION * 0.5 * parity / (sine * sine)


def split(values):
    high = values.astype(jnp.bfloat16)
    rest = values - high.astype(jnp.float32)
    middle = rest.astype(jnp.bfloat16)
    low = (rest - middle.astype(jnp.float32)).astype(jnp.bfloat16)
    return high, middle, low


def kernel(
    groups, parts,
    state_hbm, cell_hbm, face_hbm, slot_hbm, index_hbm, list_hbm, count_hbm,
    out_ref,
    own, cell, face, slots, index, listed, counts,
    outgoing, incoming, solved, returned, packets, halo, table, facing, total,
    local_sem, face_sem, send_one, recv_one, send_two, recv_two, send_halo, recv_halo,
):
    inst, nvar, tiles = own.shape[0], own.shape[1], own.shape[2]
    nb = index.shape[0]
    most = listed.shape[1]
    share = tiles // groups
    count = inst * groups
    rows = inst * share
    me = lax.axis_index("inst")
    place = lax.axis_index("mesh")
    upper = lax.rem(place + 1, parts)
    lower = lax.rem(place + parts - 1, parts)

    barrier = pltpu.get_barrier_semaphore()
    for step in range(1, groups):
        pl.semaphore_signal(barrier, inc=1, device_id={"inst": lax.rem(me + step, groups)}, device_id_type=MESH)
    for other in (upper, lower):
        pl.semaphore_signal(barrier, inc=1, device_id={"mesh": other}, device_id_type=MESH)

    fetches = [
        pltpu.make_async_copy(source, target, local_sem.at[i])
        for i, (source, target) in enumerate(
            [(state_hbm, own), (list_hbm, listed), (count_hbm, counts), (slot_hbm, slots), (index_hbm, index), (cell_hbm, cell)]
        )
    ]
    for fetch in fetches:
        fetch.start()
    face_fetches = [
        pltpu.make_async_copy(face_hbm.at[n, k], face.at[n, k], face_sem.at[n * nb + k])
        for n in range(inst) for k in range(nb)
    ]
    for fetch in face_fetches:
        fetch.start()

    fetches[0].wait()
    for j in range(groups):
        for a in range(nvar):
            pieces = [own[n, a, j * share:(j + 1) * share, :] for n in range(inst)]
            outgoing[j, a, 0:rows, :] = jnp.concatenate(pieces, axis=0) if inst > 1 else pieces[0]
    pl.semaphore_wait(barrier, groups + 1)

    first = []
    for step in range(1, groups):
        target = lax.rem(me + step, groups)
        copy = pltpu.make_async_remote_copy(
            src_ref=outgoing.at[target], dst_ref=incoming.at[step],
            send_sem=send_one.at[step], recv_sem=recv_one.at[step],
            device_id={"inst": target}, device_id_type=MESH,
        )
        copy.start()
        first.append(copy)
    incoming[0] = outgoing[me]

    for n in range(inst):
        for b in range(nvar):
            column = (n * nvar + b) * LANES
            for i, piece in enumerate(split(own[n, b])):
                table[i * tiles:(i + 1) * tiles, column:column + LANES] = piece
    fetches[1].wait()
    fetches[2].wait()
    lane = lax.broadcasted_iota(jnp.int32, (most, 3 * tiles), 1) % tiles
    row = lax.broadcasted_iota(jnp.int32, (most, 3 * tiles), 0)
    wanted = listed[...].T
    picks = []
    for d in range(2):
        chosen = (lane == wanted[:, d:d + 1]) & (row < counts[0:1, d:d + 1])
        picks.append(jnp.where(chosen, 1.0, 0.0))
    pick = jnp.concatenate(picks, axis=0).astype(jnp.bfloat16)
    picked = jnp.dot(pick, table[0:3 * tiles, :], preferred_element_type=jnp.float32)
    for d in range(2):
        for n in range(inst):
            for b in range(nvar):
                column = (n * nvar + b) * LANES
                packets[d, n, b] = picked[d * most:(d + 1) * most, column:column + LANES]
    halos = []
    for d, other in ((1, upper), (0, lower)):
        copy = pltpu.make_async_remote_copy(
            src_ref=packets.at[d], dst_ref=halo.at[1 - d],
            send_sem=send_halo.at[d], recv_sem=recv_halo.at[1 - d],
            device_id={"mesh": other}, device_id_type=MESH,
        )
        copy.start()
        halos.append(copy)

    fetches[3].wait()
    width = 3 * (tiles + 2 * most)
    lane = lax.broadcasted_iota(jnp.int32, (tiles, width), 1)
    lane = jnp.where(lane < 3 * tiles, lane % tiles, tiles + (lane - 3 * tiles) % (2 * most))
    slot = slots[...].T
    chooser = jnp.concatenate(
        [jnp.where(lane == slot[:, k:k + 1], 1.0, 0.0).astype(jnp.bfloat16) for k in range(nb)], axis=0
    )

    fetches[5].wait()
    for start in range(0, tiles, ROWS):
        part = slice(start, start + ROWS)
        for n in range(inst):
            values = [own[n, b, part, :] for b in range(nvar)]
            for a in range(nvar):
                term = cell[n, a, 0, part, :] * values[0]
                for b in range(1, nvar):
                    term += cell[n, a, b, part, :] * values[b]
                total[n, a, part, :] = term

    place_row = lax.broadcasted_iota(jnp.int32, (rows, LANES), 0)
    weights = {}

    def weight(distance, shift):
        key = (distance % groups, shift)
        if key not in weights:
            values = [
                spectral_coefficient(distance * inst + i - (i + shift) % inst, count) for i in range(inst)
            ]
            made = jnp.full((rows, LANES), values[-1], jnp.float32)
            for i in range(inst - 2, -1, -1):
                made = jnp.where(place_row < (i + 1) * share, values[i], made)
            weights[key] = made
        return weights[key]

    for copy in first:
        copy.wait_recv()
    for a in range(nvar):
        sources = []
        for step in range(groups):
            value = incoming[step, a, 0:rows, :]
            turned = [value]
            for shift in range(1, inst):
                turned.append(jnp.concatenate([value[shift * share:], value[:shift * share]], axis=0))
            sources.append(turned)
        for ahead in range(groups):
            sums = None
            for step in range(groups):
                for shift in range(inst):
                    term = weight(ahead + step, shift) * sources[step][shift]
                    sums = term if sums is None else sums + term
            solved[ahead, a, 0:rows, :] = sums
    second = []
    for ahead in range(1, groups):
        target = lax.rem(me + ahead, groups)
        copy = pltpu.make_async_remote_copy(
            src_ref=solved.at[ahead], dst_ref=returned.at[me],
            send_sem=send_two.at[ahead], recv_sem=recv_two.at[ahead],
            device_id={"inst": target}, device_id_type=MESH,
        )
        copy.start()
        second.append(copy)
    returned[me] = solved[0]

    for copy in halos:
        copy.wait_recv()
    for n in range(inst):
        for b in range(nvar):
            column = (n * nvar + b) * LANES
            both = jnp.concatenate([halo[0, n, b], halo[1, n, b]], axis=0)
            for i, piece in enumerate(split(both)):
                top = 3 * tiles + i * 2 * most
                table[top:top + 2 * most, column:column + LANES] = piece
    facing[...] = jnp.dot(chooser, table[...], preferred_element_type=jnp.float32)
    fetches[4].wait()
    for fetch in face_fetches:
        fetch.wait()

    def octet(o, carry):
        part = pl.ds(pl.multiple_of(o * ROWS, ROWS), ROWS)
        for n in range(inst):
            sums = [total[n, a, part, :] for a in range(nvar)]
            for k in range(nb):
                cells = index[k, part, :]
                where = pl.ds(pl.multiple_of(k * tiles + o * ROWS, ROWS), ROWS)
                for b in range(nvar):
                    column = (n * nvar + b) * LANES
                    value = jnp.take_along_axis(
                        facing[where, column:column + LANES], cells, axis=1, mode="promise_in_bounds"
                    )
                    for a in range(nvar):
                        sums[a] += face[n, k, a, b, part, :] * value
            for a in range(nvar):
                total[n, a, part, :] = sums[a]
        return carry

    lax.fori_loop(0, tiles // ROWS, octet, 0)

    for copy in second:
        copy.wait_recv()
    each = ROWS // share
    for n in range(inst):
        for a in range(nvar):
            for o in range(tiles // ROWS):
                pieces = [returned[o * each + i, a, n * share:(n + 1) * share, :] for i in range(each)]
                part = slice(o * ROWS, (o + 1) * ROWS)
                out_ref[n, a, part, :] = total[n, a, part, :] + jnp.concatenate(pieces, axis=0)
    for copy in first + halos + second:
        copy.wait_send()


def shards(groups, parts, state, cell_block, face_block, neighbor, face_cell, send_list, send_count):
    inst, tiles, nvar, lanes = state.shape
    nb = neighbor.shape[1]
    most = send_list.shape[2]
    operands = (
        jnp.transpose(state, (0, 2, 1, 3)),
        jnp.transpose(cell_block, (0, 2, 3, 1, 4)),
        jnp.transpose(face_block, (0, 2, 3, 4, 1, 5)),
        jnp.transpose(neighbor),
        jnp.transpose(face_cell, (1, 0, 2)),
        send_list[0],
        send_count,
    )
    packed = (groups, nvar, ROWS, lanes)
    dma = pltpu.SemaphoreType.DMA
    scratch = [pltpu.VMEM(x.shape, x.dtype) for x in operands] + [
        pltpu.VMEM(packed, jnp.float32),
        pltpu.VMEM(packed, jnp.float32),
        pltpu.VMEM(packed, jnp.float32),
        pltpu.VMEM(packed, jnp.float32),
        pltpu.VMEM((2, inst, nvar, most, lanes), jnp.float32),
        pltpu.VMEM((2, inst, nvar, most, lanes), jnp.float32),
        pltpu.VMEM((3 * (tiles + 2 * most), inst * nvar * lanes), jnp.bfloat16),
        pltpu.VMEM((nb * tiles, inst * nvar * lanes), jnp.float32),
        pltpu.VMEM((inst, nvar, tiles, lanes), jnp.float32),
        dma((6,)), dma((inst * nb,)),
        dma((groups,)), dma((groups,)), dma((groups,)), dma((groups,)),
        dma((2,)), dma((2,)),
    ]
    product = pl.pallas_call(
        functools.partial(kernel, groups, parts),
        out_shape=jax.ShapeDtypeStruct((inst, nvar, tiles, lanes), jnp.float32),
        in_specs=[pl.BlockSpec(memory_space=pl.ANY)] * len(operands),
        out_specs=pl.BlockSpec(memory_space=pltpu.VMEM),
        scratch_shapes=scratch,
        compiler_params=pltpu.CompilerParams(
            collective_id=0, has_side_effects=True, vmem_limit_bytes=56 * 1024 * 1024
        ),
    )(*operands)
    return jnp.transpose(product, (0, 2, 1, 3))


def solution(mesh):
    placed = (
        P("inst", "mesh", None, None),
        P("inst", "mesh", None, None, None),
        P("inst", "mesh", None, None, None, None),
        P("mesh", None),
        P("mesh", None, None),
        P("mesh", None, None),
        P("mesh", None),
    )
    return jax.shard_map(
        functools.partial(shards, mesh.shape["inst"], mesh.shape["mesh"]),
        mesh=mesh, in_specs=placed, out_specs=P("inst", "mesh", None, None), check_vma=False,
    )
```

time: 240 us -> 16.1 us (0.07)
  local copies, waits for them, and re-layouts: 205 us -> 1.59 us
  Pallas kernels: 0 us -> 14.3 us
  between operations: 13.6 us -> 0.01 us
  other arithmetic: 7.34 us -> 0 us
  waiting for transfers between devices: 5.15 us -> 0 us
  starting transfers between devices: 5.05 us -> 0 us
  matrix products: 2.93 us -> 0 us
    gather x4 -> x0, local copies, waits for them, and re-layouts: 199 us -> none  [the longest x2 196 us: fetch(): facing = jnp.take(flattened, indices, axis=2)]
    pallas_call x0 -> x1, Pallas kernels: none -> 14.3 us  [shards(): pl.pallas_call(functools.partial(kernel, groups, parts), out_shape=jax.Sh...]
    ppermute x2 -> x0, starting transfers between devices: 5.05 us -> none  [from_behind(): return lax.ppermute(value, axis, pairs)]
    reshape x2 -> x0, local copies, waits for them, and re-layouts: 4.63 us -> none  [the longest x1 4.54 us: fetch(): jnp.transpose(buffer, (0, 2, 1, 3))]
    ppermute x2 -> x0, waiting for transfers between devices: 4.42 us -> none  [from_behind(): return lax.ppermute(value, axis, pairs)]
    reduce_sum x2 -> x0, other arithmetic: 3.23 us -> none  [the longest x1 3.14 us: couple(): return jnp.sum(blocks * facing[:, :, :, None], axis=(2, 4))]
    dot_general x1 -> x0, matrix products: 2.93 us -> none  [shards(): jnp.einsum('nm,mtac->ntac', columns, piece, precision=lax.Precision.HIGHEST)]
  transfers between devices with their start and end apart: 3 -> 0, of which waited for: 1 -> 0; matrix products, arithmetic and copies ran while one was open for 89% -> 0% of each run, Pallas kernels for 0% -> 0%
where the time goes in v1:
time: 16.1 us; the launch traced here: 15.9 us
  Pallas kernels  14.3 us (89%)
  local copies, waits for them, and re-layouts  1.59 us (10%)
    pallas_call x1, Pallas kernels, shards(): pl.pallas_call(functools.partial(kernel, groups, parts), out_shape=jax.Sh...  14.3 us
    unnamed x1, local copies, waits for them, and re-layouts  1.59 us

profile of v1, /device:TPU:0, one launch (start us, length us, event | category | flops | bytes accessed | tf_op | source)
XLA Modules:
  0.0 15.9 jit_solution(665116211753337607)
XLA Ops:
  0.0 14.3 %shard_map.73 = f32[2,5,32,128]{3,2,1,0:T(8,128)} custom-call(f32[2,5,32,128]{3,2,1,0:T(8,128)} %bitcast.10, f32[2,5,5,32,128]{4,3,2,1,0:T(8,128)} %bitcast.8, f32[2,6,5,5,32,128]{5,4,3,2,1,0:T(8,128)} %bitcast.7, s32[6,32]{1,0:T(8,128)} %bitcast.12, s32[6,32,128]{2,1,0:T(8,128)} %bitcast.11, s32[2,8]{1,0:T(2,128)} %bitcast.13, s32[1,2]{1,0:T(1,128)} %count_hbm.1), custom_call_target="tpu_custom_call" | custom-call | tf_op jit(solution)/shard_map/pallas_call | solution.py:265
  14.3 1.6 %copy.9 = f32[2,32,5,128]{3,1,2,0:T(8,128)} copy(f32[2,32,5,128]{3,1,2,0:T(8,128)} %bitcast.9) | data formatting | bytes 327680

commit v2 on v1

--- a/solution.py
+++ b/solution.py
@@ -264,7 +264,7 @@
     ]
     product = pl.pallas_call(
         functools.partial(kernel, groups, parts),
-        out_shape=jax.ShapeDtypeStruct((inst, nvar, tiles, lanes), jnp.float32),
+        out_shape=pltpu.VMEM((inst, nvar, tiles, lanes), jnp.float32),
         in_specs=[pl.BlockSpec(memory_space=pl.ANY)] * len(operands),
         out_specs=pl.BlockSpec(memory_space=pltpu.VMEM),
         scratch_shapes=scratch,

time: 16.1 us -> 14.5 us (0.901)
  local copies, waits for them, and re-layouts: 1.59 us -> 0.67 us
  Pallas kernels: 14.3 us -> 13.7 us
    unnamed x1, local copies, waits for them, and re-layouts: 1.59 us -> 0.67 us
    pallas_call x1, Pallas kernels: 14.3 us -> 13.7 us  [shards(): pl.pallas_call(functools.partial(kernel, groups, parts), out_shape=pltpu....]
where the time goes in v2:
time: 14.5 us; the launch traced here: 14.3 us
  Pallas kernels  13.7 us (94%)
  local copies, waits for them, and re-layouts  0.67 us (5%)
    pallas_call x1, Pallas kernels, shards(): pl.pallas_call(functools.partial(kernel, groups, parts), out_shape=pltpu....  13.7 us
    unnamed x1, local copies, waits for them, and re-layouts  0.67 us

profile of v2, /device:TPU:0, one launch (start us, length us, event | category | flops | bytes accessed | tf_op | source)
XLA Modules:
  0.0 14.3 jit_solution(7677079638080092241)
XLA Ops:
  0.0 13.7 %shard_map.73 = f32[2,5,32,128]{3,2,1,0:T(8,128)S(1)} custom-call(f32[2,5,32,128]{3,2,1,0:T(8,128)} %bitcast.10, f32[2,5,5,32,128]{4,3,2,1,0:T(8,128)} %bitcast.9, f32[2,6,5,5,32,128]{5,4,3,2,1,0:T(8,128)} %bitcast.8, s32[6,32]{1,0:T(8,128)} %bitcast.12, s32[6,32,128]{2,1,0:T(8,128)} %bitcast.11, s32[2,8]{1,0:T(2,128)} %bitcast.13, s32[1,2]{1,0:T(1,128)} %count_hbm.1), custom_call_target="tpu_custom_call" | custom-call | tf_op jit(solution)/shard_map/pallas_call | solution.py:265
  13.7 0.7 %copy.9 = f32[2,32,5,128]{3,1,2,0:T(8,128)} copy(f32[2,32,5,128]{3,1,2,0:T(8,128)S(1)} %bitcast.7) | data formatting | bytes 327680

commit v3 on v2

--- a/solution.py
+++ b/solution.py
@@ -79,16 +79,18 @@
             outgoing[j, a, 0:rows, :] = jnp.concatenate(pieces, axis=0) if inst > 1 else pieces[0]
     pl.semaphore_wait(barrier, groups + 1)
 
+    cuts = ((0, 2), (2, nvar))
     first = []
-    for step in range(1, groups):
-        target = lax.rem(me + step, groups)
-        copy = pltpu.make_async_remote_copy(
-            src_ref=outgoing.at[target], dst_ref=incoming.at[step],
-            send_sem=send_one.at[step], recv_sem=recv_one.at[step],
-            device_id={"inst": target}, device_id_type=MESH,
-        )
-        copy.start()
-        first.append(copy)
+    for c, (low, high) in enumerate(cuts):
+        for step in range(1, groups):
+            target = lax.rem(me + step, groups)
+            copy = pltpu.make_async_remote_copy(
+                src_ref=outgoing.at[target, low:high], dst_ref=incoming.at[step, low:high],
+                send_sem=send_one.at[c, step], recv_sem=recv_one.at[c, step],
+                device_id={"inst": target}, device_id_type=MESH,
+            )
+            copy.start()
+            first.append(copy)
     incoming[0] = outgoing[me]
 
     for n in range(inst):
@@ -145,11 +147,15 @@
     place_row = lax.broadcasted_iota(jnp.int32, (rows, LANES), 0)
     weights = {}
 
-    def weight(distance, shift):
-        key = (distance % groups, shift)
+    half = groups // 2
+
+    def weight(distance, shift, sign):
+        key = (distance % groups, shift, sign)
         if key not in weights:
+            offsets = [distance * inst + i - (i + shift) % inst for i in range(inst)]
             values = [
-                spectral_coefficient(distance * inst + i - (i + shift) % inst, count) for i in range(inst)
+                0.5 * (spectral_coefficient(x, count) + sign * spectral_coefficient(x + count // 2, count))
+                for x in offsets
             ]
             made = jnp.full((rows, LANES), values[-1], jnp.float32)
             for i in range(inst - 2, -1, -1):
@@ -157,33 +163,39 @@
             weights[key] = made
         return weights[key]
 
-    for copy in first:
-        copy.wait_recv()
-    for a in range(nvar):
-        sources = []
-        for step in range(groups):
-            value = incoming[step, a, 0:rows, :]
-            turned = [value]
-            for shift in range(1, inst):
-                turned.append(jnp.concatenate([value[shift * share:], value[:shift * share]], axis=0))
-            sources.append(turned)
-        for ahead in range(groups):
-            sums = None
+    second = []
+    for c, (low, high) in enumerate(cuts):
+        for copy in first[c * (groups - 1):(c + 1) * (groups - 1)]:
+            copy.wait_recv()
+        for a in range(low, high):
+            sources = []
             for step in range(groups):
-                for shift in range(inst):
-                    term = weight(ahead + step, shift) * sources[step][shift]
-                    sums = term if sums is None else sums + term
-            solved[ahead, a, 0:rows, :] = sums
-    second = []
-    for ahead in range(1, groups):
-        target = lax.rem(me + ahead, groups)
-        copy = pltpu.make_async_remote_copy(
-            src_ref=solved.at[ahead], dst_ref=returned.at[me],
-            send_sem=send_two.at[ahead], recv_sem=recv_two.at[ahead],
-            device_id={"inst": target}, device_id_type=MESH,
-        )
-        copy.start()
-        second.append(copy)
+                value = incoming[step, a, 0:rows, :]
+                turned = [value]
+                for shift in range(1, inst):
+                    turned.append(jnp.concatenate([value[shift * share:], value[:shift * share]], axis=0))
+                sources.append(turned)
+            sums = [[x + y for x, y in zip(sources[i], sources[i + half])] for i in range(half)]
+            differences = [[x - y for x, y in zip(sources[i], sources[i + half])] for i in range(half)]
+            for ahead in range(half):
+                even = odd = None
+                for step in range(half):
+                    for shift in range(inst):
+                        plus = weight(ahead + step, shift, 1.0) * sums[step][shift]
+                        minus = weight(ahead + step, shift, -1.0) * differences[step][shift]
+                        even = plus if even is None else even + plus
+                        odd = minus if odd is None else odd + minus
+                solved[ahead, a, 0:rows, :] = even + odd
+                solved[ahead + half, a, 0:rows, :] = even - odd
+        for ahead in range(1, groups):
+            target = lax.rem(me + ahead, groups)
+            copy = pltpu.make_async_remote_copy(
+                src_ref=solved.at[ahead, low:high], dst_ref=returned.at[me, low:high],
+                send_sem=send_two.at[c, ahead], recv_sem=recv_two.at[c, ahead],
+                device_id={"inst": target}, device_id_type=MESH,
+            )
+            copy.start()
+            second.append(copy)
     returned[me] = solved[0]
 
     for copy in halos:
@@ -259,7 +271,7 @@
         pltpu.VMEM((nb * tiles, inst * nvar * lanes), jnp.float32),
         pltpu.VMEM((inst, nvar, tiles, lanes), jnp.float32),
         dma((6,)), dma((inst * nb,)),
-        dma((groups,)), dma((groups,)), dma((groups,)), dma((groups,)),
+        dma((2, groups)), dma((2, groups)), dma((2, groups)), dma((2, groups)),
         dma((2,)), dma((2,)),
     ]
     product = pl.pallas_call(

time: 14.5 us -> 14.4 us (level)
  no operation moved by 1% of the time
where the time goes in v3:
time: 14.4 us; the launch traced here: 14.2 us
  Pallas kernels  13.6 us (94%)
  local copies, waits for them, and re-layouts  0.67 us (5%)
    pallas_call x1, Pallas kernels, shards(): pl.pallas_call(functools.partial(kernel, groups, parts), out_shape=pltpu....  13.6 us
    unnamed x1, local copies, waits for them, and re-layouts  0.67 us

profile of v3, /device:TPU:0, one launch (start us, length us, event | category | flops | bytes accessed | tf_op | source)
XLA Modules:
  0.0 14.2 jit_solution(13575799099748691556)
XLA Ops:
  0.0 13.6 %shard_map.73 = f32[2,5,32,128]{3,2,1,0:T(8,128)S(1)} custom-call(f32[2,5,32,128]{3,2,1,0:T(8,128)} %bitcast.10, f32[2,5,5,32,128]{4,3,2,1,0:T(8,128)} %bitcast.9, f32[2,6,5,5,32,128]{5,4,3,2,1,0:T(8,128)} %bitcast.8, s32[6,32]{1,0:T(8,128)} %bitcast.12, s32[6,32,128]{2,1,0:T(8,128)} %bitcast.11, s32[2,8]{1,0:T(2,128)} %bitcast.13, s32[1,2]{1,0:T(1,128)} %count_hbm.1), custom_call_target="tpu_custom_call" | custom-call | tf_op jit(solution)/shard_map/pallas_call | solution.py:277
  13.6 0.7 %copy.9 = f32[2,32,5,128]{3,1,2,0:T(8,128)} copy(f32[2,32,5,128]{3,1,2,0:T(8,128)S(1)} %bitcast.7) | data formatting | bytes 327680
